TPU v7x, 32 devices: a whole 2x2x4 slice. The times are simulated.
32 devices in a mesh: dp: 8 (over y, x, core), tensor: 4 (over z).
Axes of the slice: x: 2, y: 2, z: 4, core: 2. Of those that a mesh axis runs over, the one named last changes fastest.
Arguments:
- inner_x: bfloat16 [2048, 8192], P(('dp', 'tensor')), parts along dimension 0, may hold values from -6 to 6
- inner_bc: bfloat16 [2048, 2048], P(('dp', 'tensor')), parts along dimension 0, may hold values from -6 to 6
- step_raw: bfloat16 [2048, 128], P(('dp', 'tensor')), parts along dimension 0, may hold values from -5 to 5
- conv_state_x: bfloat16 [24, 8192], P('dp', 'tensor'), parts along dimension 0, may hold values from -6 to 6
- conv_state_bc: bfloat16 [24, 2048], P('dp'), parts along dimension 0, may hold values from -6 to 6
- conv_weight_x: bfloat16 [4, 8192], P(None, 'tensor'), may hold values from -3 to 3
- conv_bias_x: bfloat16 [8192], P('tensor'), may hold values from -3 to 3
- conv_weight_bc: bfloat16 [4, 2048], replicated, may hold values from -3 to 3
- conv_bias_bc: bfloat16 [2048], replicated, may hold values from -3 to 3
- step_bias: float32 [128], P('tensor'), may hold values from -4 to -2
- decay_rate: float32 [128], P('tensor'), may hold values from 0 to 1, as said below
- skip_gain: float32 [128], P('tensor'), may hold values from 0.5 to 1.5
- norm_weight: bfloat16 [8192], replicated, may hold values from 0.5 to 1.5
- scan_state: float32 [1024, 64, 256], P(('dp', 'tensor')), parts along dimension 0, may hold values from -3 to 3
Outputs:
- normed: bfloat16 [2048, 8192], P(('dp', 'tensor')), parts along dimension 0
- final_state: float32 [1024, 64, 256], P(('dp', 'tensor')), parts along dimension 0
- conv_tail_x: bfloat16 [24, 8192], P('dp', 'tensor'), parts along dimension 0
- conv_tail_bc: bfloat16 [24, 2048], P('dp', 'tensor'), parts along dimension 0
There are 8 independent parts, one for each index of `dp`. A program takes and returns all parts, laid end to end along the dimension named above; an argument that names none is the same for every part. Nothing has to cross between parts.
Inputs may be any that keep to these rules, and one draw needn't show every extreme that they name: decay_rate lies between 2 / 256 and 1 / 2.
All inputs are finite; a program needn't handle non-finite values.
Results may differ from a plain program's by a relative error of at most 0.0051.
Values may be sent and summed in bfloat16 or wider, within the bound.
A program may use at most 64 MiB of HBM per device.

v0:
```python
import jax
import jax.numpy as jnp
from jax import lax
from jax.sharding import PartitionSpec as P

HEAD_DIM = 64
STATE = 256
GROUPS = 4
CONV_K = 4
INNER = 8192


EPSILON = 1e-05


def causal_conv(raw, state, weight, bias):
    length = raw.shape[0]
    padded = jnp.concatenate([state.astype(jnp.float32), raw.astype(jnp.float32)], axis=0)
    total = jnp.zeros(raw.shape, jnp.float32) + bias.astype(jnp.float32)[None, :]
    for kernel_tap in range(CONV_K):
        total = (
            total
            + weight[kernel_tap].astype(jnp.float32)[None, :]
            * padded[kernel_tap : kernel_tap + length]
        )
    return jax.nn.silu(total).astype(jnp.bfloat16)


def state_mix(
    mixed_x, mixed_bc, step_raw, step_bias, decay_rate, skip_gain, scan_state, groups_here
):
    length = mixed_x.shape[0]
    heads_here = step_raw.shape[1]
    per_group = heads_here // groups_here
    step_size = jax.nn.softplus(step_raw.astype(jnp.float32) + step_bias[None, :])
    running = jnp.cumsum(-step_size * decay_rate[None, :], axis=0)
    halves = mixed_bc.reshape(length, groups_here, 2, STATE)
    input_map = halves[:, :, 0, :]
    output_map = halves[:, :, 1, :]
    step_cols = jnp.transpose(step_size)
    running_cols = jnp.transpose(running)
    query_rows = min(512, length)
    pieces = []
    for row_start in range(0, length, query_rows):
        row_stop = row_start + query_rows
        scores = jnp.einsum(
            "tgn,sgn->gts",
            output_map[row_start:row_stop],
            input_map[:row_stop],
            preferred_element_type=jnp.float32,
        )
        causal = row_start + lax.broadcasted_iota(
            jnp.int32, (query_rows, row_stop), 0
        ) >= lax.broadcasted_iota(jnp.int32, (query_rows, row_stop), 1)
        visible = mixed_x[:row_stop]

        def one_head(
            item,
            scores=scores,
            causal=causal,
            visible=visible,
            row_start=row_start,
            row_stop=row_stop,
        ):
            head_index, step_head, running_head = item
            group_scores = lax.dynamic_index_in_dim(
                scores, head_index // per_group, 0, keepdims=False
            )
            log_gap = running_head[row_start:row_stop, None] - running_head[None, :row_stop]
            decayed = jnp.exp(jnp.where(causal, log_gap, 0.0))
            weights = jnp.where(
                causal, group_scores * decayed * step_head[None, :row_stop], 0.0
            ).astype(jnp.bfloat16)
            values = lax.dynamic_slice_in_dim(visible, head_index * HEAD_DIM, HEAD_DIM, 1)
            return jnp.dot(weights, values, preferred_element_type=jnp.float32)

        local_mix = lax.map(
            one_head, (jnp.arange(heads_here, dtype=jnp.int32), step_cols, running_cols)
        )
        pieces.append(
            jnp.transpose(local_mix, (1, 0, 2)).reshape(query_rows, heads_here * HEAD_DIM)
        )
    local_all = jnp.concatenate(pieces, axis=0)
    grouped_state = scan_state.reshape(groups_here, per_group, HEAD_DIM, STATE)
    carried = jnp.einsum(
        "tgn,ghpn->tghp",
        output_map.astype(jnp.float32),
        grouped_state,
        precision=lax.Precision.HIGHEST,
    )
    carried = carried.reshape(length, heads_here, HEAD_DIM) * jnp.exp(running)[:, :, None]
    channels = mixed_x.reshape(length, heads_here, HEAD_DIM).astype(jnp.float32)
    mixed = (
        local_all.reshape(length, heads_here, HEAD_DIM)
        + carried
        + skip_gain[None, :, None] * channels
    )
    mixed_y = mixed.reshape(length, heads_here * HEAD_DIM).astype(jnp.bfloat16)
    tail_decay = jnp.exp(running[length - 1][None, :] - running) * step_size
    weighted = (
        input_map.astype(jnp.float32)[:, :, None, :]
        * tail_decay.reshape(length, groups_here, per_group)[:, :, :, None]
    ).astype(jnp.bfloat16)
    gathered_in = jnp.einsum(
        "tghp,tghn->ghpn",
        mixed_x.reshape(length, groups_here, per_group, HEAD_DIM),
        weighted,
        preferred_element_type=jnp.float32,
    )
    final = (
        jnp.exp(running[length - 1]).reshape(groups_here, per_group)[:, :, None, None]
        * grouped_state
        + gathered_in
    )
    return (mixed_y, final.reshape(heads_here, HEAD_DIM, STATE))


def group_norm(mixed_y, norm_weight):
    rows = mixed_y.shape[0]
    values = mixed_y.astype(jnp.float32).reshape(rows, GROUPS, INNER // GROUPS)
    mean_square = jnp.mean(values * values, axis=2, keepdims=True)
    scaled = (values * lax.rsqrt(mean_square + EPSILON)).reshape(rows, INNER)
    return (scaled * norm_weight.astype(jnp.float32)[None, :]).astype(jnp.bfloat16)


def local(
    inner_x,
    inner_bc,
    step_raw,
    conv_state_x,
    conv_state_bc,
    conv_weight_x,
    conv_bias_x,
    conv_weight_bc,
    conv_bias_bc,
    step_bias,
    decay_rate,
    skip_gain,
    norm_weight,
    scan_state,
):
    tensor_count = lax.axis_size("tensor")
    device_rank = lax.axis_index("tensor")
    token_rows = inner_x.shape[0]
    heads_here = step_bias.shape[0]
    group_width = 2 * STATE
    groups_here = max(1, GROUPS // tensor_count)
    first_group = device_rank * GROUPS // tensor_count
    column_start = first_group * group_width
    x_send = inner_x.reshape(token_rows, tensor_count, heads_here * HEAD_DIM)
    step_send = step_raw.reshape(token_rows, tensor_count, heads_here)
    whole_bc = lax.all_gather(inner_bc, "tensor", axis=0, tiled=True)
    head_x, head_step = (
        lax.all_to_all(x_send, "tensor", split_axis=1, concat_axis=0, tiled=True),
        lax.all_to_all(step_send, "tensor", split_axis=1, concat_axis=0, tiled=True),
    )
    head_bc = lax.dynamic_slice_in_dim(whole_bc, column_start, groups_here * group_width, 1)
    length = head_x.shape[0]
    head_x = head_x.reshape(length, heads_here * HEAD_DIM)
    head_step = head_step.reshape(length, heads_here)
    own_state_bc = lax.dynamic_slice_in_dim(
        conv_state_bc, column_start, groups_here * group_width, 1
    )
    own_weight_bc = lax.dynamic_slice_in_dim(
        conv_weight_bc, column_start, groups_here * group_width, 1
    )
    own_bias_bc = lax.dynamic_slice_in_dim(conv_bias_bc, column_start, groups_here * group_width, 0)
    mixed_x = causal_conv(head_x, conv_state_x, conv_weight_x, conv_bias_x)
    mixed_bc = causal_conv(head_bc, own_state_bc, own_weight_bc, own_bias_bc)
    mixed_y, final_state = state_mix(
        mixed_x, mixed_bc, head_step, step_bias, decay_rate, skip_gain, scan_state, groups_here
    )
    token_y = lax.all_to_all(mixed_y, "tensor", split_axis=0, concat_axis=1, tiled=True)
    normed = group_norm(token_y, norm_weight)
    tail_x = head_x[length - CONV_K + 1 :]
    columns_here = 2 * GROUPS * STATE // tensor_count
    offset = device_rank * columns_here - column_start
    tail_bc = lax.dynamic_slice_in_dim(head_bc[length - CONV_K + 1 :], offset, columns_here, 1)
    return (normed, final_state, tail_x, tail_bc)


def solution(mesh):
    return jax.shard_map(
        local,
        mesh=mesh,
        in_specs=(
            P(("dp", "tensor"), None),
            P(("dp", "tensor"), None),
            P(("dp", "tensor"), None),
            P("dp", "tensor"),
            P("dp", None),
            P(None, "tensor"),
            P("tensor"),
            P(),
            P(),
            P("tensor"),
            P("tensor"),
            P("tensor"),
            P(),
            P(("dp", "tensor"), None, None),
        ),
        out_specs=(
            P(("dp", "tensor"), None),
            P(("dp", "tensor"), None, None),
            P("dp", "tensor"),
            P("dp", "tensor"),
        ),
        check_vma=False,
    )
```

profile of v0, /device:TPU:0, one launch (start us, length us, event | category | flops | bytes accessed | tf_op | source)
XLA Modules:
  0.0 241.6 jit_solution(5700607315440728388)
XLA Ops:
  9.5 6.3 %all-to-all-start = ((bf16[4,2,1024]{2,1,0:T(2,128)(2,1)}), bf16[4,2,1024]{2,1,0:T(2,128)(2,1)S(1)}, u32[]{:S(2)}, u32[]{:S(2)}) async-start(bf16[4,2,1024]{2,1,0:T(2,128)(2,1)} %reshape.136), calls=%async_computation | async-start | bytes 32768 | tf_op jit(solution)/shard_map/all_to_all | solution.py:155
  18.6 2.4 copy.77
  21.4 4.7 %all-to-all-start.1 = ((bf16[64,4,2048]{2,0,1:T(8,128)(2,1)}), bf16[64,4,2048]{2,0,1:T(8,128)(2,1)S(1)}, u32[]{:S(2)}, u32[]{:S(2)}) async-start(bf16[64,4,2048]{2,0,1:T(8,128)(2,1)} %bitcast.106), calls=%async_computation.1 | async-start | bytes 2097152 | tf_op jit(solution)/shard_map/all_to_all | solution.py:154
  28.1 23.9 %all-gather.2.cloned.1.call-done = bf16[256,2048]{1,0:T(8,128)(2,1)} async-done(((bf16[64,2048]{1,0:T(8,128)(2,1)}), bf16[256,2048]{1,0:T(8,128)(2,1)}) %all-gather.2.cloned.1.call-update) | async-done | bytes 1048592 | tf_op jit(solution)/shard_map/all_gather | solution.py:152
  55.1 7.8 %all-to-all-done.1 = bf16[64,4,2048]{2,0,1:T(8,128)(2,1)S(1)} async-done(((bf16[64,4,2048]{2,0,1:T(8,128)(2,1)}), bf16[64,4,2048]{2,0,1:T(8,128)(2,1)S(1)}, u32[]{:S(2)}, u32[]{:S(2)}) %all-to-all-start.1) | async-done | bytes 1048608 | tf_op jit(solution)/shard_map/all_to_all | solution.py:154
  63.9 2.2 multiply_convert_fusion.3
  68.2 125.5 %while.12 = (s32[]{:T(128)}, f32[32,256,64]{1,2,0:T(8,128)}, f32[1,256,256]{2,1,0:T(8,128)}, f32[32,256]{1,0:T(8,128)S(1)}, f32[32,256]{1,0:T(8,128)S(1)}, /*ind...) while((s32[]{:T(128)}, f32[32,256,64]{1,2,0:T(8,128)}, ...), condition=%wide.region_3.4_spmd.clone.clone, body=%wide.region_2.3_spmd.clone.clone.sunk | while | flops 8847366 | bytes 401071 | solution.py:77
  70.3 1.9 fusion.55
  74.2 1.9 fusion.55
  78.1 1.9 fusion.55
  86.0 1.9 fusion.55
  89.9 1.9 fusion.55
  97.7 1.9 fusion.55
  101.6 1.9 fusion.55
  105.6 1.9 fusion.55
  109.5 1.9 fusion.55
  117.3 1.9 fusion.55
  121.2 1.9 fusion.55
  129.1 1.9 fusion.55
  133.0 1.9 fusion.55
  136.9 1.9 fusion.55
  140.9 1.9 fusion.55
  144.8 1.9 fusion.55
  148.7 1.9 fusion.55
  152.6 1.9 fusion.55
  160.5 1.9 fusion.55
  193.7 3.8 %fusion.31 = bf16[256,32,64]{0,2,1:T(8,128)(2,1)} fusion(f32[32,256,64]{1,2,0:T(8,128)} %get-tuple-element.49, bf16[256,32,64]{0,2,1:T(8,128)(2,1)S(1)} %bitcast.117, f32[32,64,256]{2,1,0:T(8,128)S(1)} %copy-done.1, f32[32]{0:T(128)} %param.27, f32[256,32]{0,1:T(8,128)S(1)} %get-tuple-element.116, bf16[256,1,2,256]{0,3,2,1:T(8,128)(2,1)S(1)} %bitcast.122), kind=kOutput, calls=%fused_computation.41 | convolution fusion | flops 1613758464 | bytes 6455424 | tf_op jit(solution)/shard_map/tgn,ghpn->tghp/dot_general | solution.py:85
  197.5 3.3 %reshape.133 = bf16[4,64,2048]{1,0,2:T(4,128)(2,1)S(1)} reshape(bf16[256,32,64]{0,2,1:T(8,128)(2,1)} %fusion.31) | data formatting | bytes 2097152 | tf_op jit(solution)/shard_map/convert_element_type | solution.py:98
  200.9 2.3 copy.60
  203.2 3.6 %all-to-all-start.2 = ((bf16[4,64,2048]{2,1,0:T(8,128)(2,1)}), bf16[4,64,2048]{2,1,0:T(8,128)(2,1)S(1)}, u32[]{:S(2)}, u32[]{:S(2)}) async-start(bf16[4,64,2048]{2,1,0:T(8,128)(2,1)} %copy.60), calls=%async_computation.2 | async-start | bytes 2097152 | tf_op jit(solution)/shard_map/all_to_all | solution.py:173
  209.3 3.9 %multiply_add_fusion = f32[32,64,256]{2,1,0:T(8,128)} fusion(f32[32,64,256]{2,1,0:T(8,128)} %param.29, bf16[256,32,64]{0,2,1:T(8,128)(2,1)S(1)} %bitcast.118, f32[256,32]{0,1:T(8,128)S(1)} %get-tuple-element.114, f32[256,256]{1,0:T(8,128)S(1)} %copy.58, f32[32]{0:T(128)S(1)} %exp.32), kind=kOutput, calls=%fused_computation.42 | convolution fusion | flops 273678336 | bytes 5537920 | tf_op jit(solution)/shard_map/tghp,tghn->ghpn/dot_general | solution.py:104
  213.1 19.7 %all-to-all-done.2 = bf16[4,64,2048]{2,1,0:T(8,128)(2,1)S(1)} async-done(((bf16[4,64,2048]{2,1,0:T(8,128)(2,1)}), bf16[4,64,2048]{2,1,0:T(8,128)(2,1)S(1)}, u32[]{:S(2)}, u32[]{:S(2)}) %all-to-all-start.2) | async-done | bytes 1048608 | tf_op jit(solution)/shard_map/all_to_all | solution.py:173
  (147 shorter events, 84.8 us)
Async XLA Ops:
  7.2 8.6 %copy-start = (bf16[3,2048]{1,0:T(4,128)(2,1)S(1)}, bf16[3,2048]{1,0:T(4,128)(2,1)}, u32[]{:S(2)}) copy-start(bf16[3,2048]{1,0:T(4,128)(2,1)} %param.20) | copy-start | bytes 36868
  7.2 13.8 %copy-start.5 = (bf16[3,2048]{1,0:T(4,128)(2,1)S(1)}, bf16[3,2048]{1,0:T(4,128)(2,1)}, u32[]{:S(2)}) copy-start(bf16[3,2048]{1,0:T(4,128)(2,1)} %param.19) | copy-start | bytes 36868
  7.2 13.8 %copy-start.7 = (bf16[2048]{0:T(1024)(128)(2,1)S(1)}, bf16[2048]{0:T(1024)(128)(2,1)}, u32[]{:S(2)}) copy-start(bf16[2048]{0:T(1024)(128)(2,1)} %param.22) | copy-start | bytes 12292
  7.2 44.9 %all-gather.2.cloned.1.call-start = ((), (), s32[]{:S(2)}) async-start(), calls=%async_computation.3 | async-start | bytes 1310720 | tf_op jit(solution)/shard_map/all_gather | solution.py:152
  9.5 11.9 %all-to-all-start = ((bf16[4,2,1024]{2,1,0:T(2,128)(2,1)}), bf16[4,2,1024]{2,1,0:T(2,128)(2,1)S(1)}, u32[]{:S(2)}, u32[]{:S(2)}) async-start(bf16[4,2,1024]{2,1,0:T(2,128)(2,1)} %reshape.136), calls=%async_computation | async-start | bytes 32768 | tf_op jit(solution)/shard_map/all_to_all | solution.py:155
  18.6 7.8 %copy-start.8 = (f32[32]{0:T(128)S(1)}, f32[32]{0:T(128)}, u32[]{:S(2)}) copy-start(f32[32]{0:T(128)} %param.25) | copy-start | bytes 388
  18.6 7.8 %copy-start.11 = (f32[32]{0:T(128)S(1)}, f32[32]{0:T(128)}, u32[]{:S(2)}) copy-start(f32[32]{0:T(128)} %param.26) | copy-start | bytes 388
  21.4 41.5 %all-to-all-start.1 = ((bf16[64,4,2048]{2,0,1:T(8,128)(2,1)}), bf16[64,4,2048]{2,0,1:T(8,128)(2,1)S(1)}, u32[]{:S(2)}, u32[]{:S(2)}) async-start(bf16[64,4,2048]{2,0,1:T(8,128)(2,1)} %bitcast.106), calls=%async_computation.1 | async-start | bytes 2097152 | tf_op jit(solution)/shard_map/all_to_all | solution.py:154
  27.6 0.6 copy-start.9
  53.2 10.1 %copy-start.3 = (bf16[256,512]{0,1:T(8,128)(2,1)}, bf16[256,512]{0,1:T(8,128)(2,1)S(1)}, u32[]{:S(2)}) copy-start(bf16[256,512]{0,1:T(8,128)(2,1)S(1)} %copy.62) | copy-start | bytes 786436
  62.9 1.0 copy-start.2
  66.1 127.6 %copy-start.1 = (f32[32,64,256]{2,1,0:T(8,128)S(1)}, f32[32,64,256]{2,1,0:T(8,128)}, u32[]{:S(2)}) copy-start(f32[32,64,256]{2,1,0:T(8,128)} %param.29) | copy-start | bytes 6291460
  200.8 6.0 %copy-start.6 = (bf16[8192]{0:T(1024)(128)(2,1)S(1)}, bf16[8192]{0:T(1024)(128)(2,1)}, u32[]{:S(2)}) copy-start(bf16[8192]{0:T(1024)(128)(2,1)} %param.28) | copy-start | bytes 49156
  200.9 6.0 %copy-start.10 = (f32[32]{0:T(128)S(1)}, f32[32]{0:T(128)}, u32[]{:S(2)}) copy-start(f32[32]{0:T(128)} %copy-done.9) | copy-start | bytes 388
  203.2 3.7 %copy-start.4 = (bf16[256,512]{0,1:T(8,128)(2,1)S(1)}, bf16[256,512]{0,1:T(8,128)(2,1)}, u32[]{:S(2)}) copy-start(bf16[256,512]{0,1:T(8,128)(2,1)} %copy-done.3) | copy-start | bytes 786436
  203.2 29.7 %all-to-all-start.2 = ((bf16[4,64,2048]{2,1,0:T(8,128)(2,1)}), bf16[4,64,2048]{2,1,0:T(8,128)(2,1)S(1)}, u32[]{:S(2)}, u32[]{:S(2)}) async-start(bf16[4,64,2048]{2,1,0:T(8,128)(2,1)} %copy.60), calls=%async_computation.2 | async-start | bytes 2097152 | tf_op jit(solution)/shard_map/all_to_all | solution.py:173
Sparse Core Ops, SparseCore 0:
  9.6 42.4 all-gather.1
where the time goes:
time: 244 us; the launch traced here: 242 us
  matrix products  68.7 us (28%)
  local copies, waits for them, and re-layouts  59.9 us (25%)
  waiting for transfers between devices  52.6 us (22%)
  loops' own time  22.8 us (9%)
  starting transfers between devices  14.7 us (6%)
  between operations  14.3 us (6%)
  other arithmetic  8.65 us (4%)
    dot_general x32, matrix products, one_head(): return jnp.dot(weights, values, preferred_element_type=jnp.float32)  60 us
    dynamic_slice x64, local copies, waits for them, and re-layouts, state_mix(): lax.map(one_head, (jnp.arange(heads_here, dtype=jnp.int32), step_cols, ru...  42.7 us
    all_gather x1, waiting for transfers between devices, local(): whole_bc = lax.all_gather(inner_bc, 'tensor', axis=0, tiled=True)  23.9 us
    another operation x1, loops' own time, state_mix(): lax.map(one_head, (jnp.arange(heads_here, dtype=jnp.int32), step_cols, ru...  22.8 us
    all_to_all x1, waiting for transfers between devices, local(): lax.all_to_all(mixed_y, 'tensor', split_axis=0, concat_axis=1, tiled=True)  19.7 us
    all_to_all x1, waiting for transfers between devices, local(): lax.all_to_all(x_send, 'tensor', split_axis=1, concat_axis=0, tiled=True)  7.81 us
    all_to_all x1, starting transfers between devices, local(): lax.all_to_all(step_send, 'tensor', split_axis=1, concat_axis=0, tiled=True)  6.32 us
    convert_element_type x2, local copies, waits for them, and re-layouts, state_mix(): mixed_y = mixed.reshape(length, heads_here * HEAD_DIM).astype(jnp.bfloat16)  5.64 us
  transfers between devices with their start and end apart: 4, of which 4 were waited for; matrix products, arithmetic and copies ran while one was open for 7% of the time, Pallas kernels for 0%

commit v1 on v0

v1 whole, which is shorter than its diff:
```python
import functools
import math

import jax
import jax.numpy as jnp
from jax import lax
from jax.experimental import pallas as pl
from jax.experimental.pallas import tpu as pltpu
from jax.sharding import PartitionSpec as P

HEAD_DIM = 64
STATE = 256
GROUPS = 4
CONV_K = 4
EPSILON = 1e-05
LOG2E = math.log2(math.e)
CHUNK = 512
PAIR = 2 * HEAD_DIM
BLOCK = 256
MESH = pl.DeviceIdType.MESH
F32 = jnp.float32
BF16 = jnp.bfloat16
HIGHEST = lax.Precision.HIGHEST


def dot_nt(a, b, precision=None):
    return lax.dot_general(
        a, b, (((1,), (1,)), ((), ())), precision=precision, preferred_element_type=F32
    )


def dot_tn(a, b):
    return lax.dot_general(a, b, (((0,), (0,)), ((), ())), preferred_element_type=F32)


def silu(total):
    half = 0.5 * total
    return half + half * jnp.tanh(half)


def column_of(row):
    width = row.shape[1]
    eye = lax.broadcasted_iota(jnp.int32, (width, width), 0) == lax.broadcasted_iota(
        jnp.int32, (width, width), 1
    )
    return jnp.sum(jnp.where(eye, jnp.broadcast_to(row, (width, width)), 0.0), axis=1, keepdims=True)


def kernel(
    n,
    chunk,
    x_ref,
    bc_ref,
    step_ref,
    state_x_ref,
    state_bc_ref,
    weight_x_ref,
    bias_x_ref,
    weight_bc_ref,
    bias_bc_ref,
    step_bias_ref,
    decay_ref,
    skip_ref,
    norm_ref,
    scan_ref,
    normed_ref,
    final_ref,
    tail_x_ref,
    tail_bc_ref,
    xg,
    bcg,
    stg,
    ysend,
    yrecv,
    scan,
    fout,
    nout,
    conv_rows,
    maps,
    masked_scores,
    run_cols,
    gap_cols,
    gap_rows,
    skip_lanes,
    small_send,
    small_recv,
    x_send,
    x_recv,
    y_send,
    y_recv,
    scan_sem,
    fout_sem,
    nout_sem,
):
    me = lax.axis_index("tensor")
    rows = x_ref.shape[0]
    length = n * rows
    width = xg.shape[1]
    chunks = width // chunk
    chunk_heads = chunk // HEAD_DIM
    heads = width // HEAD_DIM
    group_width = 2 * STATE
    blocks = length // BLOCK
    group = me * GROUPS // n

    def ahead(i):
        return lax.rem(me + i, n)

    def behind(i):
        return lax.rem(me + n - i, n)

    def row_span(device):
        return pl.ds(pl.multiple_of(device * rows, rows), rows)

    def chunk_span(base, k):
        return pl.ds(pl.multiple_of(base + k * chunk, chunk), chunk)

    def group_span(device):
        start = (device * GROUPS // n) * group_width
        return pl.ds(pl.multiple_of(start, group_width), group_width)

    def bc_copy(i, peer, source):
        src, dst = bc_ref.at[:, group_span(peer)], bcg.at[row_span(source), :]
        if i == 0:
            return pltpu.make_async_copy(src, dst, small_recv.at[0, 0])
        return pltpu.make_async_remote_copy(
            src, dst, small_send.at[0, i], small_recv.at[0, i], {"tensor": peer}, MESH
        )

    def step_copy(i, peer, source):
        src, dst = step_ref, stg.at[row_span(source), :]
        if i == 0:
            return pltpu.make_async_copy(src, dst, small_recv.at[1, 0])
        return pltpu.make_async_remote_copy(
            src, dst, small_send.at[1, i], small_recv.at[1, i], {"tensor": peer}, MESH
        )

    def x_copy(i, k, peer, source):
        src = x_ref.at[:, chunk_span(peer * width, k)]
        dst = xg.at[row_span(source), chunk_span(0, k)]
        if i == 0:
            return pltpu.make_async_copy(src, dst, x_recv.at[0, k])
        return pltpu.make_async_remote_copy(
            src, dst, x_send.at[i, k], x_recv.at[i, k], {"tensor": peer}, MESH
        )

    def y_copy(i, k, peer, source):
        src = ysend.at[row_span(peer), chunk_span(0, k)]
        dst = yrecv.at[:, chunk_span(source * width, k)]
        if i == 0:
            return pltpu.make_async_copy(src, dst, y_recv.at[0, k])
        return pltpu.make_async_remote_copy(
            src, dst, y_send.at[i, k], y_recv.at[i, k], {"tensor": peer}, MESH
        )

    def scan_copy(k):
        return pltpu.make_async_copy(
            scan_ref.at[chunk_span(0, k), :], scan.at[chunk_span(0, k), :], scan_sem.at[k]
        )

    def fout_copy(k):
        return pltpu.make_async_copy(
            fout.at[chunk_span(0, k), :], final_ref.at[chunk_span(0, k), :], fout_sem.at[k]
        )

    def start_to_all(copy):
        for i in range(n):
            copy(i, ahead(i), me).start()

    def arrive_from_all(copy):
        for i in range(n):
            if i == 0:
                copy(0, me, me).wait()
            else:
                copy(i, ahead(i), behind(i)).wait_recv()

    barrier = pltpu.get_barrier_semaphore()
    for i in range(1, n):
        pl.semaphore_signal(barrier, inc=1, device_id={"tensor": ahead(i)}, device_id_type=MESH)
    pl.semaphore_wait(barrier, n - 1)

    start_to_all(step_copy)
    start_to_all(bc_copy)
    for k in range(chunks):
        start_to_all(lambda i, peer, source: x_copy(i, k, peer, source))
    for k in range(chunks):
        scan_copy(k).start()

    arrive_from_all(step_copy)
    lanes_all = stg.shape[1]
    pick = (
        lax.broadcasted_iota(jnp.int32, (heads, lanes_all), 1)
        == lax.broadcasted_iota(jnp.int32, (heads, lanes_all), 0) + me * heads
    ).astype(BF16)
    bias_row, decay_row = step_bias_ref[...], decay_ref[...]
    bias_col, decay_col = column_of(bias_row), column_of(decay_row)
    below = (
        lax.broadcasted_iota(jnp.int32, (BLOCK, BLOCK), 0)
        >= lax.broadcasted_iota(jnp.int32, (BLOCK, BLOCK), 1)
    )
    lower = below.astype(F32)
    base_cols = jnp.zeros((1, heads), F32)
    base_rows = jnp.zeros((heads, 1), F32)
    for b in range(blocks):
        span = slice(b * BLOCK, (b + 1) * BLOCK)
        raw = stg[span, :]
        step = jnp.log1p(jnp.exp(dot_nt(raw, pick) + bias_row))
        run = base_cols - jnp.dot(
            lower, step * decay_row, precision=HIGHEST, preferred_element_type=F32
        )
        base_cols = run[BLOCK - 1 :, :]
        gap = run * LOG2E - jnp.log(step) * LOG2E
        for k in range(chunks):
            run_cols[k, span, :] = run[:, k * chunk_heads : (k + 1) * chunk_heads] * LOG2E
            gap_cols[k, span, :] = gap[:, k * chunk_heads : (k + 1) * chunk_heads]
        step = jnp.log1p(jnp.exp(dot_nt(pick, raw) + bias_col))
        run = base_rows - dot_nt(step * decay_col, lower, precision=HIGHEST)
        base_rows = run[:, BLOCK - 1 :]
        gap = run * LOG2E - jnp.log(step) * LOG2E
        for k in range(chunks):
            gap_rows[k, :, span] = gap[k * chunk_heads : (k + 1) * chunk_heads, :]
    spread = (
        lax.broadcasted_iota(jnp.int32, (heads, width), 1) // HEAD_DIM
        == lax.broadcasted_iota(jnp.int32, (heads, width), 0)
    ).astype(F32)
    skip_lanes[...] = jnp.dot(
        jnp.broadcast_to(skip_ref[...], (8, heads)),
        spread,
        precision=HIGHEST,
        preferred_element_type=F32,
    )

    def convolve(raw, state, weight, bias):
        conv_rows[8 - CONV_K + 1 : 8, :] = state.astype(F32)
        conv_rows[8:, :] = raw.astype(F32)
        total = jnp.broadcast_to(bias.astype(F32), (length, PAIR))
        for tap in range(CONV_K):
            start = 8 - CONV_K + 1 + tap
            total = total + weight[tap : tap + 1, :].astype(F32) * conv_rows[start : start + length, :]
        return silu(total).astype(BF16)

    arrive_from_all(bc_copy)
    for j in range(group_width // PAIR):
        cols = pl.ds(pl.multiple_of(group * group_width + j * PAIR, PAIR), PAIR)
        maps[:, j * PAIR : (j + 1) * PAIR] = convolve(
            bcg[:, j * PAIR : (j + 1) * PAIR],
            state_bc_ref[:, cols],
            weight_bc_ref[:, cols],
            bias_bc_ref[:, cols],
        )
    for q in range(blocks):
        here = slice(q * BLOCK, (q + 1) * BLOCK)
        for s in range(q + 1):
            there = slice(s * BLOCK, (s + 1) * BLOCK)
            scores = dot_nt(maps[here, STATE:], maps[there, :STATE])
            masked_scores[here, there] = jnp.where(below, scores, 0.0) if s == q else scores
    tail_cols = tail_bc_ref.shape[1]
    offset = pl.multiple_of(me * tail_cols - group * group_width, tail_cols)
    tail_bc_ref[...] = bcg[length - 16 :, pl.ds(offset, tail_cols)][16 - CONV_K + 1 :, :]

    first_lanes = lax.broadcasted_iota(jnp.int32, (BLOCK, PAIR), 1) < HEAD_DIM
    first_rows = lax.broadcasted_iota(jnp.int32, (PAIR, 1), 0) < HEAD_DIM

    def one_chunk(k, carry):
        arrive_from_all(lambda i, peer, source: x_copy(i, k, peer, source))
        scan_copy(k).wait()
        for j in range(chunk // PAIR):
            cols = pl.ds(pl.multiple_of(k * chunk + j * PAIR, PAIR), PAIR)
            mixed = convolve(
                xg[:, cols], state_x_ref[:, cols], weight_x_ref[:, cols], bias_x_ref[:, cols]
            )
            old = scan[cols, :]
            high = old.astype(BF16)
            low = (old - high.astype(F32)).astype(BF16)
            ends = [run_cols[k, length - 1 :, 2 * j + h : 2 * j + h + 1] for h in (0, 1)]
            gained = None
            for q in range(blocks):
                here = slice(q * BLOCK, (q + 1) * BLOCK)
                values = mixed[here, :].astype(F32)
                out = maps[here, STATE:]
                run = [
                    jnp.broadcast_to(run_cols[k, here, 2 * j + h : 2 * j + h + 1], (BLOCK, PAIR))
                    for h in (0, 1)
                ]
                total = (dot_nt(out, high) + dot_nt(out, low)) * jnp.where(
                    first_lanes, jnp.exp2(run[0]), jnp.exp2(run[1])
                )
                total = total + skip_lanes[0:1, cols] * values
                for s in range(q + 1):
                    there = slice(s * BLOCK, (s + 1) * BLOCK)
                    for h in (0, 1):
                        row = gap_rows[k, 2 * j + h : 2 * j + h + 1, there]
                        wide = jnp.concatenate([run[h]] * (BLOCK // PAIR), axis=1)
                        decayed = jnp.exp2(jnp.minimum(wide - row, 64.0))
                        weights = (masked_scores[here, there] * decayed).astype(BF16)
                        keep = first_lanes if h == 0 else jnp.logical_not(first_lanes)
                        seen = jnp.where(keep, mixed[there, :].astype(F32), 0.0).astype(BF16)
                        total = total + jnp.dot(weights, seen, preferred_element_type=F32)
                ysend[here, cols] = total.astype(BF16)
                tails = [
                    jnp.exp2(ends[h] - gap_cols[k, here, 2 * j + h : 2 * j + h + 1]) for h in (0, 1)
                ]
                tailed = (values * jnp.where(first_lanes, tails[0], tails[1])).astype(BF16)
                part = dot_tn(tailed, maps[here, :STATE])
                gained = part if gained is None else gained + part
            fade = jnp.where(first_rows, jnp.exp2(ends[0]), jnp.exp2(ends[1]))
            fout[cols, :] = fade * old + gained
        start_to_all(lambda i, peer, source: y_copy(i, k, peer, source))
        fout_copy(k).start()
        return carry

    lax.fori_loop(0, chunks, one_chunk, 0)
    tail_x_ref[...] = xg[length - 16 :, :][16 - CONV_K + 1 :, :]

    members = max(1, n // GROUPS)
    norm_width = nout.shape[1] // GROUPS

    def arrive(i):
        for k in range(chunks):
            if i == 0:
                y_copy(0, k, me, me).wait()
            else:
                y_copy(i, k, ahead(i), behind(i)).wait_recv()

    def nout_copy(q, span):
        return pltpu.make_async_copy(nout.at[:, span], normed_ref.at[:, span], nout_sem.at[q])

    if members > 1:
        for i in range(n):
            arrive(i)
    spans = []
    for q in range(GROUPS):
        if members == 1:
            arrive(q)
            start = behind(q) * norm_width
        else:
            start = q * norm_width
        span = pl.ds(pl.multiple_of(start, norm_width), norm_width)
        values = yrecv[:, span].astype(F32)
        square = jnp.mean(values * values, axis=1, keepdims=True)
        scaled = values * lax.rsqrt(square + EPSILON)
        nout[:, span] = (scaled * norm_ref[:, span].astype(F32)).astype(BF16)
        nout_copy(q, span).start()
        spans.append(span)

    for i in range(1, n):
        step_copy(i, ahead(i), me).wait_send()
        bc_copy(i, ahead(i), me).wait_send()
        for k in range(chunks):
            x_copy(i, k, ahead(i), me).wait_send()
            y_copy(i, k, ahead(i), me).wait_send()
    for k in range(chunks):
        fout_copy(k).wait()
    for q in range(GROUPS):
        nout_copy(q, spans[q]).wait()


def local(
    inner_x,
    inner_bc,
    step_raw,
    conv_state_x,
    conv_state_bc,
    conv_weight_x,
    conv_bias_x,
    conv_weight_bc,
    conv_bias_bc,
    step_bias,
    decay_rate,
    skip_gain,
    norm_weight,
    scan_state,
):
    n = lax.axis_size("tensor")
    rows, inner = inner_x.shape
    heads = step_bias.shape[0]
    width = heads * HEAD_DIM
    length = n * rows
    chunk = min(CHUNK, width)
    chunks = width // chunk
    chunk_heads = chunk // HEAD_DIM
    group_width = 2 * STATE
    tail_cols = inner_bc.shape[1] // n
    dma = pltpu.SemaphoreType.DMA
    hbm = pl.BlockSpec(memory_space=pl.ANY)
    vmem = pl.BlockSpec(memory_space=pltpu.VMEM)
    outs = pl.pallas_call(
        functools.partial(kernel, n, chunk),
        out_shape=(
            jax.ShapeDtypeStruct((rows, inner), BF16),
            jax.ShapeDtypeStruct((width, STATE), F32),
            jax.ShapeDtypeStruct((CONV_K - 1, width), BF16),
            jax.ShapeDtypeStruct((CONV_K - 1, tail_cols), BF16),
        ),
        in_specs=[hbm] * 3 + [vmem] * 10 + [hbm],
        out_specs=(hbm, hbm, vmem, vmem),
        scratch_shapes=[
            pltpu.VMEM((length, width), BF16),
            pltpu.VMEM((length, group_width), BF16),
            pltpu.VMEM((length, step_raw.shape[1]), BF16),
            pltpu.VMEM((length, width), BF16),
            pltpu.VMEM((rows, inner), BF16),
            pltpu.VMEM((width, STATE), F32),
            pltpu.VMEM((width, STATE), F32),
            pltpu.VMEM((rows, inner), BF16),
            pltpu.VMEM((length + 8, PAIR), F32),
            pltpu.VMEM((length, group_width), BF16),
            pltpu.VMEM((length, length), F32),
            pltpu.VMEM((chunks, length, chunk_heads), F32),
            pltpu.VMEM((chunks, length, chunk_heads), F32),
            pltpu.VMEM((chunks, chunk_heads, length), F32),
            pltpu.VMEM((8, width), F32),
            dma((2, n)),
            dma((2, n)),
            dma((n, chunks)),
            dma((n, chunks)),
            dma((n, chunks)),
            dma((n, chunks)),
            dma((chunks,)),
            dma((chunks,)),
            dma((GROUPS,)),
        ],
        compiler_params=pltpu.CompilerParams(
            collective_id=0, has_side_effects=True, vmem_limit_bytes=48 * 1024 * 1024
        ),
    )(
        inner_x,
        inner_bc,
        step_raw,
        conv_state_x,
        conv_state_bc,
        conv_weight_x,
        conv_bias_x.reshape(1, -1),
        conv_weight_bc,
        conv_bias_bc.reshape(1, -1),
        step_bias.reshape(1, -1),
        decay_rate.reshape(1, -1),
        skip_gain.reshape(1, -1),
        norm_weight.reshape(1, -1),
        scan_state.reshape(width, STATE),
    )
    normed, final_state, tail_x, tail_bc = outs
    return (normed, final_state.reshape(heads, HEAD_DIM, STATE), tail_x, tail_bc)


def solution(mesh):
    return jax.shard_map(
        local,
        mesh=mesh,
        in_specs=(
            P(("dp", "tensor"), None),
            P(("dp", "tensor"), None),
            P(("dp", "tensor"), None),
            P("dp", "tensor"),
            P("dp", None),
            P(None, "tensor"),
            P("tensor"),
            P(),
            P(),
            P("tensor"),
            P("tensor"),
            P("tensor"),
            P(),
            P(("dp", "tensor"), None, None),
        ),
        out_specs=(
            P(("dp", "tensor"), None),
            P(("dp", "tensor"), None, None),
            P("dp", "tensor"),
            P("dp", "tensor"),
        ),
        check_vma=False,
    )
```

time: 244 us -> 72.7 us (0.30)
  matrix products: 68.7 us -> 0 us
  Pallas kernels: 0 us -> 58 us
  waiting for transfers between devices: 52.6 us -> 0 us
  local copies, waits for them, and re-layouts: 59.9 us -> 13.3 us
  loops' own time: 22.8 us -> 0 us
  starting transfers between devices: 14.7 us -> 0 us
  between operations: 14.3 us -> 0.66 us
  other arithmetic: 8.65 us -> 0 us
    dot_general x35 -> x0, matrix products: 68.7 us -> none  [the longest x32 60 us: one_head(): return jnp.dot(weights, values, preferred_element_type=jnp.float32)]
    pallas_call x0 -> x1, Pallas kernels: none -> 58 us  [local(): pl.pallas_call(functools.partial(kernel, n, chunk), out_shape=(jax.ShapeD...]
    dynamic_slice x66 -> x0, local copies, waits for them, and re-layouts: 43.6 us -> none  [the longest x64 42.7 us: state_mix(): lax.map(one_head, (jnp.arange(heads_here, dtype=jnp.int32), step_cols, ru...]
    all_to_all x3 -> x0, waiting for transfers between devices: 27.9 us -> none  [the longest x1 19.7 us: local(): lax.all_to_all(mixed_y, 'tensor', split_axis=0, concat_axis=1, tiled=True)]
    all_gather x1 -> x0, waiting for transfers between devices: 23.9 us -> none  [local(): whole_bc = lax.all_gather(inner_bc, 'tensor', axis=0, tiled=True)]
    another operation x1 -> x0, loops' own time: 22.8 us -> none  [state_mix(): lax.map(one_head, (jnp.arange(heads_here, dtype=jnp.int32), step_cols, ru...]
    all_to_all x3 -> x0, starting transfers between devices: 14.7 us -> none  [the longest x1 6.32 us: local(): lax.all_to_all(step_send, 'tensor', split_axis=1, concat_axis=0, tiled=True)]
    convert_element_type x5 -> x0, local copies, waits for them, and re-layouts: 7.42 us -> none  [the longest x2 5.64 us: state_mix(): mixed_y = mixed.reshape(length, heads_here * HEAD_DIM).astype(jnp.bfloat16)]
  transfers between devices with their start and end apart: 4 -> 0, of which waited for: 4 -> 0; matrix products, arithmetic and copies ran while one was open for 7% -> 0% of each run, Pallas kernels for 0% -> 0%
where the time goes in v1:
time: 72.7 us; the launch traced here: 71.9 us
  Pallas kernels  58 us (80%)
  local copies, waits for them, and re-layouts  13.3 us (18%)
    pallas_call x1, Pallas kernels, local(): pl.pallas_call(functools.partial(kernel, n, chunk), out_shape=(jax.ShapeD...  58 us
    unnamed x24, local copies, waits for them, and re-layouts  11.2 us

profile of v1, /device:TPU:0, one launch (start us, length us, event | category | flops | bytes accessed | tf_op | source)
XLA Modules:
  0.0 71.9 jit_solution(15830269967834539577)
XLA Ops:
  0.6 0.7 reshape.32.bias_x_ref
  1.3 0.7 reshape.33.bias_bc_ref
  2.0 0.7 %reshape.37.norm_ref = bf16[1,8192]{1,0:T(2,128)(2,1)S(1)} reshape(bf16[8192]{0:T(1024)(128)(2,1)} %param.26) | data formatting | bytes 32768 | tf_op jit(solution)/shard_map/reshape | solution.py:439
  2.8 0.0 copy-start
  2.8 1.2 %copy-done = bf16[64,8192]{1,0:T(8,128)(2,1)S(1)} copy-done((bf16[64,8192]{1,0:T(8,128)(2,1)S(1)}, bf16[64,8192]{1,0:T(8,128)(2,1)}, u32[]{:S(2)}) %copy-start) | copy-done | bytes 1048600
  4.0 0.0 copy-start.1
  4.0 0.9 %copy-done.1 = bf16[64,2048]{1,0:T(8,128)(2,1)S(1)} copy-done((bf16[64,2048]{1,0:T(8,128)(2,1)S(1)}, bf16[64,2048]{1,0:T(8,128)(2,1)}, u32[]{:S(2)}) %copy-start.1) | copy-done | bytes 262168
  4.9 0.0 copy-start.2
  4.9 0.7 copy-done.2
  5.7 0.0 copy-start.3
  5.7 0.7 copy-done.3
  6.4 0.0 copy-start.4
  6.4 0.7 copy-done.4
  7.1 0.0 copy-start.5
  7.1 0.7 copy-done.5
  7.8 0.0 copy-start.6
  7.8 0.7 copy-done.6
  8.5 0.0 copy-start.7
  8.5 0.7 copy-done.7
  9.2 0.0 copy-start.8
  9.2 0.7 copy-done.8
  9.8 0.0 copy-start.9
  9.8 0.7 copy-done.9
  10.5 58.0 %shard_map.165 = (bf16[64,8192]{1,0:T(8,128)(2,1)S(1)}, f32[2048,256]{1,0:T(8,128)S(1)}, bf16[3,2048]{1,0:T(4,128)(2,1)S(1)}, bf16[3,512]{1,0:T(4,128)(2,1)S(1)}) custom-call(bf16[64,8192]{1,0:T(8,128)(2,1)S(1)} %copy-done, bf16[64,2048]{1,0:T(8,128)(2,1)S(1)} %copy-done.1, bf16[64,128]{1,0:T(8,128)(2,1)S(1)} %copy-done.2, bf16[3,2048]{1,0:T(4,128)(2,1)S(1)} %copy-done.3, ...), custom_call_target="tpu_custom_call" | custom-call | tf_op jit(solution)/shard_map/pallas_call | solution.py:387
  68.5 1.0 %copy.22 = bf16[64,8192]{1,0:T(8,128)(2,1)} copy(bf16[64,8192]{1,0:T(8,128)(2,1)S(1)} %get-tuple-element.16) | data formatting | bytes 2097152
  69.4 1.3 %copy.23 = f32[32,64,256]{2,1,0:T(8,128)} copy(f32[32,64,256]{2,1,0:T(8,128)S(1)} %bitcast.5) | data formatting | bytes 4194304
  70.7 0.6 copy.24
  71.4 0.6 copy.25
Async XLA Ops:
  2.8 1.2 %copy-start = (bf16[64,8192]{1,0:T(8,128)(2,1)S(1)}, bf16[64,8192]{1,0:T(8,128)(2,1)}, u32[]{:S(2)}) copy-start(bf16[64,8192]{1,0:T(8,128)(2,1)} %x_ref.1) | copy-start | bytes 3145732
  4.0 0.9 %copy-start.1 = (bf16[64,2048]{1,0:T(8,128)(2,1)S(1)}, bf16[64,2048]{1,0:T(8,128)(2,1)}, u32[]{:S(2)}) copy-start(bf16[64,2048]{1,0:T(8,128)(2,1)} %bc_ref.1) | copy-start | bytes 786436
  4.9 0.7 copy-start.2
  5.7 0.7 copy-start.3
  6.4 0.7 copy-start.4
  7.1 0.7 copy-start.5
  7.8 0.7 copy-start.6
  8.5 0.7 copy-start.7
  9.2 0.7 copy-start.8
  9.8 0.7 copy-start.9

commit v2 on v1

--- a/solution.py
+++ b/solution.py
@@ -15,6 +15,8 @@
 EPSILON = 1e-05
 LOG2E = math.log2(math.e)
 CHUNK = 512
+SPLITS = (4, 8, 1, 1)
+VMEM_LIMIT = 60 * 1024 * 1024
 PAIR = 2 * HEAD_DIM
 BLOCK = 256
 MESH = pl.DeviceIdType.MESH
@@ -52,46 +54,56 @@
     x_ref,
     bc_ref,
     step_ref,
-    state_x_ref,
-    state_bc_ref,
-    weight_x_ref,
-    bias_x_ref,
-    weight_bc_ref,
-    bias_bc_ref,
-    step_bias_ref,
-    decay_ref,
-    skip_ref,
-    norm_ref,
-    scan_ref,
-    normed_ref,
-    final_ref,
-    tail_x_ref,
-    tail_bc_ref,
-    xg,
-    bcg,
-    stg,
-    ysend,
-    yrecv,
-    scan,
-    fout,
-    nout,
-    conv_rows,
-    maps,
-    masked_scores,
-    run_cols,
-    gap_cols,
-    gap_rows,
-    skip_lanes,
-    small_send,
-    small_recv,
-    x_send,
-    x_recv,
-    y_send,
-    y_recv,
-    scan_sem,
-    fout_sem,
-    nout_sem,
+    *refs,
 ):
+    small_in = refs[:10]
+    scan_ref, normed_out, final_out, tail_x_out, tail_bc_out = refs[10:15]
+    small = refs[15:25]
+    (
+        state_x_ref,
+        state_bc_ref,
+        weight_x_ref,
+        bias_x_in,
+        weight_bc_ref,
+        bias_bc_in,
+        step_bias_ref,
+        decay_ref,
+        skip_ref,
+        norm_in,
+    ) = small
+    (
+        xg,
+        bcg,
+        stg,
+        ysend,
+        yrecv,
+        scan,
+        fout,
+        nout,
+        tail_x_ref,
+        tail_bc_ref,
+        conv_rows,
+        maps,
+        masked_scores,
+        run_cols,
+        gap_cols,
+        gap_rows,
+        skip_lanes,
+        bias_x_ref,
+        bias_bc_ref,
+        norm_ref,
+        small_send,
+        small_recv,
+        x_send,
+        x_recv,
+        y_send,
+        y_recv,
+        scan_sem,
+        local_sem,
+        fout_sem,
+        nout_sem,
+        tail_sem,
+    ) = refs[25:]
     me = lax.axis_index("tensor")
     rows = x_ref.shape[0]
     length = n * rows
@@ -103,11 +115,15 @@
     blocks = length // BLOCK
     group = me * GROUPS // n
 
-    def ahead(i):
-        return lax.rem(me + i, n)
-
-    def behind(i):
-        return lax.rem(me + n - i, n)
+    order = list(range(n // 2, n)) + list(range(1, n // 2)) + [0]
+
+    def partner(i):
+        other, bit = me, 1
+        while bit <= i:
+            if i & bit:
+                other = other + bit - 2 * bit * ((me // bit) % 2)
+            bit *= 2
+        return other
 
     def row_span(device):
         return pl.ds(pl.multiple_of(device * rows, rows), rows)
@@ -158,25 +174,37 @@
             scan_ref.at[chunk_span(0, k), :], scan.at[chunk_span(0, k), :], scan_sem.at[k]
         )
 
+    def small_copy(i):
+        return pltpu.make_async_copy(small_in[i], small[i], local_sem.at[i])
+
     def fout_copy(k):
-        return pltpu.make_async_copy(
-            fout.at[chunk_span(0, k), :], final_ref.at[chunk_span(0, k), :], fout_sem.at[k]
-        )
+        span = chunk_span(0, k)
+        return pltpu.make_async_copy(fout.at[span, :], final_out.at[span, :], fout_sem.at[k])
+
+    def nout_copy(q, span):
+        return pltpu.make_async_copy(nout.at[:, span], normed_out.at[:, span], nout_sem.at[q])
+
+    tail_copies = (
+        pltpu.make_async_copy(tail_x_ref, tail_x_out, tail_sem.at[0]),
+        pltpu.make_async_copy(tail_bc_ref, tail_bc_out, tail_sem.at[1]),
+    )
 
     def start_to_all(copy):
-        for i in range(n):
-            copy(i, ahead(i), me).start()
+        for i in order:
+            copy(i, partner(i), me).start()
 
     def arrive_from_all(copy):
         for i in range(n):
             if i == 0:
                 copy(0, me, me).wait()
             else:
-                copy(i, ahead(i), behind(i)).wait_recv()
-
+                copy(i, partner(i), partner(i)).wait_recv()
+
+    for i in range(len(small)):
+        small_copy(i).start()
     barrier = pltpu.get_barrier_semaphore()
     for i in range(1, n):
-        pl.semaphore_signal(barrier, inc=1, device_id={"tensor": ahead(i)}, device_id_type=MESH)
+        pl.semaphore_signal(barrier, inc=1, device_id={"tensor": partner(i)}, device_id_type=MESH)
     pl.semaphore_wait(barrier, n - 1)
 
     start_to_all(step_copy)
@@ -185,6 +213,12 @@
         start_to_all(lambda i, peer, source: x_copy(i, k, peer, source))
     for k in range(chunks):
         scan_copy(k).start()
+
+    for i in range(len(small)):
+        small_copy(i).wait()
+    bias_x_ref[...] = bias_x_in[...].astype(F32)
+    bias_bc_ref[...] = bias_bc_in[...].astype(F32)
+    norm_ref[...] = norm_in[...].astype(F32)
 
     arrive_from_all(step_copy)
     lanes_all = stg.shape[1]
@@ -233,7 +267,7 @@
     def convolve(raw, state, weight, bias):
         conv_rows[8 - CONV_K + 1 : 8, :] = state.astype(F32)
         conv_rows[8:, :] = raw.astype(F32)
-        total = jnp.broadcast_to(bias.astype(F32), (length, PAIR))
+        total = jnp.broadcast_to(bias, (length, PAIR))
         for tap in range(CONV_K):
             start = 8 - CONV_K + 1 + tap
             total = total + weight[tap : tap + 1, :].astype(F32) * conv_rows[start : start + length, :]
@@ -246,7 +280,7 @@
             bcg[:, j * PAIR : (j + 1) * PAIR],
             state_bc_ref[:, cols],
             weight_bc_ref[:, cols],
-            bias_bc_ref[:, cols],
+            bias_bc_ref[pl.ds(group * (group_width // PAIR) + j, 1), :],
         )
     for q in range(blocks):
         here = slice(q * BLOCK, (q + 1) * BLOCK)
@@ -267,7 +301,10 @@
         for j in range(chunk // PAIR):
             cols = pl.ds(pl.multiple_of(k * chunk + j * PAIR, PAIR), PAIR)
             mixed = convolve(
-                xg[:, cols], state_x_ref[:, cols], weight_x_ref[:, cols], bias_x_ref[:, cols]
+                xg[:, cols],
+                state_x_ref[:, cols],
+                weight_x_ref[:, cols],
+                bias_x_ref[pl.ds(k * (chunk // PAIR) + j, 1), :],
             )
             old = scan[cols, :]
             high = old.astype(BF16)
@@ -312,7 +349,11 @@
     lax.fori_loop(0, chunks, one_chunk, 0)
     tail_x_ref[...] = xg[length - 16 :, :][16 - CONV_K + 1 :, :]
 
+    for copy in tail_copies:
+        copy.start()
+
     members = max(1, n // GROUPS)
+    spans = []
     norm_width = nout.shape[1] // GROUPS
 
     def arrive(i):
@@ -320,39 +361,62 @@
             if i == 0:
                 y_copy(0, k, me, me).wait()
             else:
-                y_copy(i, k, ahead(i), behind(i)).wait_recv()
-
-    def nout_copy(q, span):
-        return pltpu.make_async_copy(nout.at[:, span], normed_ref.at[:, span], nout_sem.at[q])
+                y_copy(i, k, partner(i), partner(i)).wait_recv()
 
     if members > 1:
         for i in range(n):
             arrive(i)
-    spans = []
     for q in range(GROUPS):
         if members == 1:
             arrive(q)
-            start = behind(q) * norm_width
+            start = partner(q) * norm_width
         else:
             start = q * norm_width
         span = pl.ds(pl.multiple_of(start, norm_width), norm_width)
         values = yrecv[:, span].astype(F32)
-        square = jnp.mean(values * values, axis=1, keepdims=True)
-        scaled = values * lax.rsqrt(square + EPSILON)
-        nout[:, span] = (scaled * norm_ref[:, span].astype(F32)).astype(BF16)
+        inverse = lax.rsqrt(jnp.mean(values * values, axis=1, keepdims=True) + EPSILON)
+        first = start // PAIR
+        for j in range(norm_width // PAIR):
+            cols = pl.ds(pl.multiple_of(start + j * PAIR, PAIR), PAIR)
+            scaled = yrecv[:, cols].astype(F32) * inverse
+            nout[:, cols] = (scaled * norm_ref[pl.ds(first + j, 1), :]).astype(BF16)
         nout_copy(q, span).start()
         spans.append(span)
 
     for i in range(1, n):
-        step_copy(i, ahead(i), me).wait_send()
-        bc_copy(i, ahead(i), me).wait_send()
+        step_copy(i, partner(i), me).wait_send()
+        bc_copy(i, partner(i), me).wait_send()
         for k in range(chunks):
-            x_copy(i, k, ahead(i), me).wait_send()
-            y_copy(i, k, ahead(i), me).wait_send()
+            x_copy(i, k, partner(i), me).wait_send()
+            y_copy(i, k, partner(i), me).wait_send()
     for k in range(chunks):
         fout_copy(k).wait()
     for q in range(GROUPS):
         nout_copy(q, spans[q]).wait()
+    for copy in tail_copies:
+        copy.wait()
+
+def write_out(*refs):
+    arrive, leave = [], []
+    for i in range(4):
+        source, target, stage = refs[i], refs[4 + i], refs[8 + i]
+        size = source.shape[0] // SPLITS[i]
+        for p in range(SPLITS[i]):
+            span = pl.ds(p * size, size)
+            sem = len(arrive)
+            arrive.append(
+                pltpu.make_async_copy(source.at[span, :], stage.at[span, :], refs[12].at[sem])
+            )
+            leave.append(
+                pltpu.make_async_copy(stage.at[span, :], target.at[span, :], refs[13].at[sem])
+            )
+    for copy in arrive:
+        copy.start()
+    for first, second in zip(arrive, leave):
+        first.wait()
+        second.start()
+    for copy in leave:
+        copy.wait()
 
 
 def local(
@@ -382,19 +446,32 @@
     group_width = 2 * STATE
     tail_cols = inner_bc.shape[1] // n
     dma = pltpu.SemaphoreType.DMA
-    hbm = pl.BlockSpec(memory_space=pl.ANY)
-    vmem = pl.BlockSpec(memory_space=pltpu.VMEM)
+    hbm = pl.BlockSpec(memory_space=pltpu.HBM)
+    small = (
+        conv_state_x,
+        conv_state_bc,
+        conv_weight_x,
+        conv_bias_x.reshape(-1, PAIR),
+        conv_weight_bc,
+        conv_bias_bc.reshape(-1, PAIR),
+        step_bias.reshape(1, -1),
+        decay_rate.reshape(1, -1),
+        skip_gain.reshape(1, -1),
+        norm_weight.reshape(-1, PAIR),
+    )
+    out_shape = (
+        jax.ShapeDtypeStruct((rows, inner), BF16),
+        jax.ShapeDtypeStruct((width, STATE), F32),
+        jax.ShapeDtypeStruct((CONV_K - 1, width), BF16),
+        jax.ShapeDtypeStruct((CONV_K - 1, tail_cols), BF16),
+    )
     outs = pl.pallas_call(
         functools.partial(kernel, n, chunk),
-        out_shape=(
-            jax.ShapeDtypeStruct((rows, inner), BF16),
-            jax.ShapeDtypeStruct((width, STATE), F32),
-            jax.ShapeDtypeStruct((CONV_K - 1, width), BF16),
-            jax.ShapeDtypeStruct((CONV_K - 1, tail_cols), BF16),
-        ),
-        in_specs=[hbm] * 3 + [vmem] * 10 + [hbm],
-        out_specs=(hbm, hbm, vmem, vmem),
-        scratch_shapes=[
+        out_shape=out_shape,
+        in_specs=[hbm] * 14,
+        out_specs=(hbm,) * 4,
+        scratch_shapes=[pltpu.VMEM(a.shape, a.dtype) for a in small]
+        + [
             pltpu.VMEM((length, width), BF16),
             pltpu.VMEM((length, group_width), BF16),
             pltpu.VMEM((length, step_raw.shape[1]), BF16),
@@ -403,6 +480,8 @@
             pltpu.VMEM((width, STATE), F32),
             pltpu.VMEM((width, STATE), F32),
             pltpu.VMEM((rows, inner), BF16),
+            pltpu.VMEM(out_shape[2].shape, BF16),
+            pltpu.VMEM(out_shape[3].shape, BF16),
             pltpu.VMEM((length + 8, PAIR), F32),
             pltpu.VMEM((length, group_width), BF16),
             pltpu.VMEM((length, length), F32),
@@ -410,6 +489,9 @@
             pltpu.VMEM((chunks, length, chunk_heads), F32),
             pltpu.VMEM((chunks, chunk_heads, length), F32),
             pltpu.VMEM((8, width), F32),
+            pltpu.VMEM(small[3].shape, F32),
+            pltpu.VMEM(small[5].shape, F32),
+            pltpu.VMEM(small[9].shape, F32),
             dma((2, n)),
             dma((2, n)),
             dma((n, chunks)),
@@ -417,28 +499,30 @@
             dma((n, chunks)),
             dma((n, chunks)),
             dma((chunks,)),
+            dma((len(small),)),
             dma((chunks,)),
             dma((GROUPS,)),
+            dma((2,)),
         ],
         compiler_params=pltpu.CompilerParams(
-            collective_id=0, has_side_effects=True, vmem_limit_bytes=48 * 1024 * 1024
+            collective_id=0, has_side_effects=True, vmem_limit_bytes=VMEM_LIMIT
         ),
     )(
         inner_x,
         inner_bc,
         step_raw,
-        conv_state_x,
-        conv_state_bc,
-        conv_weight_x,
-        conv_bias_x.reshape(1, -1),
-        conv_weight_bc,
-        conv_bias_bc.reshape(1, -1),
-        step_bias.reshape(1, -1),
-        decay_rate.reshape(1, -1),
-        skip_gain.reshape(1, -1),
-        norm_weight.reshape(1, -1),
+        *small,
         scan_state.reshape(width, STATE),
     )
+    outs = pl.pallas_call(
+        write_out,
+        out_shape=out_shape,
+        in_specs=[hbm] * 4,
+        out_specs=(hbm,) * 4,
+        scratch_shapes=[pltpu.VMEM(a.shape, a.dtype) for a in out_shape]
+        + [dma((sum(SPLITS),)), dma((sum(SPLITS),))],
+        compiler_params=pltpu.CompilerParams(vmem_limit_bytes=VMEM_LIMIT),
+    )(*outs)
     normed, final_state, tail_x, tail_bc = outs
     return (normed, final_state.reshape(heads, HEAD_DIM, STATE), tail_x, tail_bc)
 

time: 72.7 us -> 62.6 us (0.86)
  local copies, waits for them, and re-layouts: 13.3 us -> 0 us
  Pallas kernels: 58 us -> 61.8 us
    unnamed x24 -> x0, local copies, waits for them, and re-layouts: 11.2 us -> none
    pallas_call x1 -> x2, Pallas kernels: 58 us -> 61.8 us  [the longest x1 58.9 us: local(): pl.pallas_call(functools.partial(kernel, n, chunk), out_shape=out_shape,...]
    reshape x3 -> x0, local copies, waits for them, and re-layouts: 2.12 us -> none  [the longest x1 0.74 us: local(): norm_weight.reshape(1, -1)]
where the time goes in v2:
time: 62.6 us; the launch traced here: 62.4 us
  Pallas kernels  61.8 us (99%)
  between operations  0.64 us (1%)
    pallas_call x1, Pallas kernels, local(): pl.pallas_call(functools.partial(kernel, n, chunk), out_shape=out_shape,...  58.9 us
    pallas_call x1, Pallas kernels, local(): pl.pallas_call(write_out, out_shape=out_shape, in_specs=[hbm] * 4, out_sp...  2.85 us

profile of v2, /device:TPU:0, one launch (start us, length us, event | category | flops | bytes accessed | tf_op | source)
XLA Modules:
  0.0 62.4 jit_solution(107188604056902888)
XLA Ops:
  0.6 58.9 %shard_map.165 = (bf16[64,8192]{1,0:T(8,128)(2,1)}, f32[2048,256]{1,0:T(8,128)}, bf16[3,2048]{1,0:T(4,128)(2,1)}, bf16[3,512]{1,0:T(4,128)(2,1)}) custom-call(bf16[64,8192]{1,0:T(8,128)(2,1)} %x_ref.1, bf16[64,2048]{1,0:T(8,128)(2,1)} %bc_ref.1, bf16[64,128]{1,0:T(8,128)(2,1)} %step_ref.1, bf16[3,2048]{1,0:T(4,128)(2,1)} %refs_0_.1, ...), custom_call_target="tpu_custom_call" | custom-call | tf_op jit(solution)/shard_map/pallas_call | solution.py:468
  59.6 2.9 %shard_map.166 = (bf16[64,8192]{1,0:T(8,128)(2,1)}, f32[2048,256]{1,0:T(8,128)}, bf16[3,2048]{1,0:T(4,128)(2,1)}, bf16[3,512]{1,0:T(4,128)(2,1)}) custom-call(bf16[64,8192]{1,0:T(8,128)(2,1)} %get-tuple-element.12.refs_0_, f32[2048,256]{1,0:T(8,128)} %get-tuple-element.13.refs_1_, bf16[3,2048]{1,0:T(4,128)(2,1)} %get-tuple-element.14.refs_2_, ...), custom_call_target="tpu_custom_call" | custom-call | tf_op jit(solution)/shard_map/pallas_call | solution.py:517

commit v3 on v2

--- a/solution.py
+++ b/solution.py
@@ -76,10 +76,8 @@
         bcg,
         stg,
         ysend,
-        yrecv,
         scan,
         fout,
-        nout,
         tail_x_ref,
         tail_bc_ref,
         conv_rows,
@@ -101,7 +99,6 @@
         scan_sem,
         local_sem,
         fout_sem,
-        nout_sem,
         tail_sem,
     ) = refs[25:]
     me = lax.axis_index("tensor")
@@ -162,7 +159,7 @@
 
     def y_copy(i, k, peer, source):
         src = ysend.at[row_span(peer), chunk_span(0, k)]
-        dst = yrecv.at[:, chunk_span(source * width, k)]
+        dst = normed_out.at[:, chunk_span(source * width, k)]
         if i == 0:
             return pltpu.make_async_copy(src, dst, y_recv.at[0, k])
         return pltpu.make_async_remote_copy(
@@ -180,9 +177,6 @@
     def fout_copy(k):
         span = chunk_span(0, k)
         return pltpu.make_async_copy(fout.at[span, :], final_out.at[span, :], fout_sem.at[k])
-
-    def nout_copy(q, span):
-        return pltpu.make_async_copy(nout.at[:, span], normed_out.at[:, span], nout_sem.at[q])
 
     tail_copies = (
         pltpu.make_async_copy(tail_x_ref, tail_x_out, tail_sem.at[0]),
@@ -352,10 +346,6 @@
     for copy in tail_copies:
         copy.start()
 
-    members = max(1, n // GROUPS)
-    spans = []
-    norm_width = nout.shape[1] // GROUPS
-
     def arrive(i):
         for k in range(chunks):
             if i == 0:
@@ -363,25 +353,8 @@
             else:
                 y_copy(i, k, partner(i), partner(i)).wait_recv()
 
-    if members > 1:
-        for i in range(n):
-            arrive(i)
-    for q in range(GROUPS):
-        if members == 1:
-            arrive(q)
-            start = partner(q) * norm_width
-        else:
-            start = q * norm_width
-        span = pl.ds(pl.multiple_of(start, norm_width), norm_width)
-        values = yrecv[:, span].astype(F32)
-        inverse = lax.rsqrt(jnp.mean(values * values, axis=1, keepdims=True) + EPSILON)
-        first = start // PAIR
-        for j in range(norm_width // PAIR):
-            cols = pl.ds(pl.multiple_of(start + j * PAIR, PAIR), PAIR)
-            scaled = yrecv[:, cols].astype(F32) * inverse
-            nout[:, cols] = (scaled * norm_ref[pl.ds(first + j, 1), :]).astype(BF16)
-        nout_copy(q, span).start()
-        spans.append(span)
+    for i in range(n):
+        arrive(i)
 
     for i in range(1, n):
         step_copy(i, partner(i), me).wait_send()
@@ -391,30 +364,50 @@
             y_copy(i, k, partner(i), me).wait_send()
     for k in range(chunks):
         fout_copy(k).wait()
-    for q in range(GROUPS):
-        nout_copy(q, spans[q]).wait()
     for copy in tail_copies:
         copy.wait()
 
 def write_out(*refs):
+    norm_in, norm_ref, norm_sem = refs[4], refs[15], refs[16]
+    norm_copy = pltpu.make_async_copy(norm_in, norm_ref, norm_sem)
+    norm_copy.start()
     arrive, leave = [], []
     for i in range(4):
-        source, target, stage = refs[i], refs[4 + i], refs[8 + i]
+        source, target, stage = refs[i], refs[5 + i], refs[9 + i]
         size = source.shape[0] // SPLITS[i]
         for p in range(SPLITS[i]):
             span = pl.ds(p * size, size)
             sem = len(arrive)
             arrive.append(
-                pltpu.make_async_copy(source.at[span, :], stage.at[span, :], refs[12].at[sem])
+                pltpu.make_async_copy(source.at[span, :], stage.at[span, :], refs[13].at[sem])
             )
             leave.append(
-                pltpu.make_async_copy(stage.at[span, :], target.at[span, :], refs[13].at[sem])
+                pltpu.make_async_copy(stage.at[span, :], target.at[span, :], refs[14].at[sem])
             )
     for copy in arrive:
         copy.start()
-    for first, second in zip(arrive, leave):
-        first.wait()
-        second.start()
+    norm_copy.wait()
+    gains = norm_ref[...].astype(F32)
+    stage = refs[9]
+    size = stage.shape[0] // SPLITS[0]
+    norm_width = stage.shape[1] // GROUPS
+    for p in range(SPLITS[0]):
+        span = slice(p * size, (p + 1) * size)
+        arrive[p].wait()
+        for q in range(GROUPS):
+            values = stage[span, q * norm_width : (q + 1) * norm_width].astype(F32)
+            inverse = lax.rsqrt(jnp.mean(values * values, axis=1, keepdims=True) + EPSILON)
+            for j in range(q * norm_width // PAIR, (q + 1) * norm_width // PAIR):
+                cols = slice(j * PAIR, (j + 1) * PAIR)
+                scaled = stage[span, cols].astype(F32) * inverse
+                stage[span, cols] = (scaled * gains[j : j + 1, :]).astype(BF16)
+        leave[p].start()
+        for k in range(SPLITS[0] + 2 * p, SPLITS[0] + 2 * p + 2):
+            arrive[k].wait()
+            leave[k].start()
+    for k in range(3 * SPLITS[0], len(arrive)):
+        arrive[k].wait()
+        leave[k].start()
     for copy in leave:
         copy.wait()
 
@@ -476,10 +469,8 @@
             pltpu.VMEM((length, group_width), BF16),
             pltpu.VMEM((length, step_raw.shape[1]), BF16),
             pltpu.VMEM((length, width), BF16),
-            pltpu.VMEM((rows, inner), BF16),
             pltpu.VMEM((width, STATE), F32),
             pltpu.VMEM((width, STATE), F32),
-            pltpu.VMEM((rows, inner), BF16),
             pltpu.VMEM(out_shape[2].shape, BF16),
             pltpu.VMEM(out_shape[3].shape, BF16),
             pltpu.VMEM((length + 8, PAIR), F32),
@@ -501,7 +492,6 @@
             dma((chunks,)),
             dma((len(small),)),
             dma((chunks,)),
-            dma((GROUPS,)),
             dma((2,)),
         ],
         compiler_params=pltpu.CompilerParams(
@@ -517,12 +507,12 @@
     outs = pl.pallas_call(
         write_out,
         out_shape=out_shape,
-        in_specs=[hbm] * 4,
+        in_specs=[hbm] * 5,
         out_specs=(hbm,) * 4,
         scratch_shapes=[pltpu.VMEM(a.shape, a.dtype) for a in out_shape]
-        + [dma((sum(SPLITS),)), dma((sum(SPLITS),))],
+        + [dma((sum(SPLITS),)), dma((sum(SPLITS),)), pltpu.VMEM(small[9].shape, BF16), dma],
         compiler_params=pltpu.CompilerParams(vmem_limit_bytes=VMEM_LIMIT),
-    )(*outs)
+    )(*outs, small[9])
     normed, final_state, tail_x, tail_bc = outs
     return (normed, final_state.reshape(heads, HEAD_DIM, STATE), tail_x, tail_bc)
 

time: 62.6 us -> 62.6 us (level)
    pallas_call x1, Pallas kernels: 58.9 us -> 58 us  [local(): pl.pallas_call(functools.partial(kernel, n, chunk), out_shape=out_shape,...]
    pallas_call x1, Pallas kernels: 2.85 us -> 3.75 us  [local(): pl.pallas_call(write_out, out_shape=out_shape, in_specs=[hbm] * 5, out_sp...]
where the time goes in v3:
time: 62.6 us; the launch traced here: 62.4 us
  Pallas kernels  61.8 us (99%)
  between operations  0.64 us (1%)
    pallas_call x1, Pallas kernels, local(): pl.pallas_call(functools.partial(kernel, n, chunk), out_shape=out_shape,...  58 us
    pallas_call x1, Pallas kernels, local(): pl.pallas_call(write_out, out_shape=out_shape, in_specs=[hbm] * 5, out_sp...  3.75 us

profile of v3, /device:TPU:0, one launch (start us, length us, event | category | flops | bytes accessed | tf_op | source)
XLA Modules:
  0.0 62.4 jit_solution(6700907635068028995)
XLA Ops:
  0.6 58.0 %shard_map.165 = (bf16[64,8192]{1,0:T(8,128)(2,1)}, f32[2048,256]{1,0:T(8,128)}, bf16[3,2048]{1,0:T(4,128)(2,1)}, bf16[3,512]{1,0:T(4,128)(2,1)}) custom-call(bf16[64,8192]{1,0:T(8,128)(2,1)} %x_ref.1, bf16[64,2048]{1,0:T(8,128)(2,1)} %bc_ref.1, bf16[64,128]{1,0:T(8,128)(2,1)} %step_ref.1, bf16[3,2048]{1,0:T(4,128)(2,1)} %refs_0_.1, ...), custom_call_target="tpu_custom_call" | custom-call | tf_op jit(solution)/shard_map/pallas_call | solution.py:461
  58.7 3.7 %shard_map.166 = (bf16[64,8192]{1,0:T(8,128)(2,1)}, f32[2048,256]{1,0:T(8,128)}, bf16[3,2048]{1,0:T(4,128)(2,1)}, bf16[3,512]{1,0:T(4,128)(2,1)}) custom-call(bf16[64,8192]{1,0:T(8,128)(2,1)} %get-tuple-element.12.refs_0_, f32[2048,256]{1,0:T(8,128)} %get-tuple-element.13.refs_1_, bf16[3,2048]{1,0:T(4,128)(2,1)} %get-tuple-element.14.refs_2_, ...), custom_call_target="tpu_custom_call" | custom-call | tf_op jit(solution)/shard_map/pallas_call | solution.py:507
